TPU v7x, 256 devices: a whole 4x4x8 slice. The times are simulated.
256 devices in a mesh: dp: 16 (over z_lo, x), col: 16 (over z_hi, y, core).
Axes of the slice: x: 4, y: 4, z: 8 (z_hi: 2, z_lo: 4; z = z_hi * 4 + z_lo), core: 2. Of those that a mesh axis runs over, the one named last changes fastest.
Arguments:
- latent: bfloat16 [32768, 512], P('dp'), may hold values from -6 to 6
- adapter_down_matrix: bfloat16 [64, 512], replicated, may hold values from -0.25 to 0.25
- output_gradient_rows: bfloat16 [32768, 32768], P('dp', 'col'), may hold values from -40 to 40
- output_sketch_factor: bfloat16 [32768, 128], P('col'), may hold values from -0.03125 to 0.03125
- rank_sketch_factor: bfloat16 [64, 64], replicated, may hold values from -0.75 to 0.75
- token_example_index: int32 [32768], P('dp'), may hold values from 0 to 127, as said below
- validation_sketches: float32 [256, 8192], P('dp', 'col'), may hold values from -6 to 6
Outputs:
- scores: float32 [128, 256], P('dp')
Inputs may be any that keep to these rules, and one draw needn't show every extreme that they name: `token_example_index`: Nondecreasing. The tokens of index i of dp carry ids from i * 8 - 1 (never below 0) to (i + 1) * 8 - 1, and every id of i's own range starts on index i; an example's tokens lie on its own index and possibly the next one.
All inputs are finite; a program needn't handle non-finite values.
Results may differ from a plain program's by a relative error of at most 0.007.
Values sent between devices are 32-bit elements; how exact they have to be, the bound alone decides.
A program may use at most 64 MiB of HBM per device.

v0:
```python
import functools
import math

import jax
import jax.numpy as jnp
from jax import lax
from jax.experimental import pallas as pl
from jax.experimental.pallas import tpu as pltpu
from jax.sharding import PartitionSpec as P

PA = 128
PB = 64
EX_DEV = 8
MESH = pl.DeviceIdType.MESH

epsilon = 1e-06

BF = jnp.bfloat16
F32 = jnp.float32

STEP = 512
OWN = EX_DEV * PB
ROWS = OWN + 2 * PB

FAR_FIRST = ((4, 0), (4, 1), (2, 0), (2, 1), (6, 0), (6, 1), (0, 1))


def nt(x, y):
    return lax.dot_general(x, y, (((1,), (1,)), ((), ())), preferred_element_type=F32)


def kernel(
    lat_h, down_h, grad_h, sketch_h, rank_h, seg_h, val_h, out_ref,
    lat, down, grad, sketch, rank, seg, masked, side, gp, gt,
    r0, a0, r1, a1, r2, r3, vg, fin, rz, fb, local_sem, lat_sem, grad_sem, vown_sem,
    s0_send, s0_recv, s1_send, s1_recv, s2_send, s2_recv, s3_send, s3_recv,
    ready, vz_send, vz_recv, vo_send, vo_recv, vx_send, vx_recv, vf_send, vf_recv, fz_send, fz_recv, fb_send, fb_recv,
):
    i = lax.axis_index("dp")
    c = lax.axis_index("col")
    zl, x = i // 4, i % 4
    zh, y, core = c // 8, (c // 2) % 4, c % 2
    p = c % 8
    below, above = (i + 15) % 16, (i + 1) % 16

    def at(dp, col):
        return {"dp": dp, "col": col}

    core_peer = at(i, zh * 8 + y * 2 + (1 - core))
    y_peer = [at(i, zh * 8 + ((y + k) % 4) * 2 + core) for k in (2, 1, 3)]
    z_peer = at(i, (1 - zh) * 8 + p)
    p_peer = [at(i, zh * 8 + (p // 2 * 2 + k) % 8 + (core + j) % 2) for k, j in FAR_FIRST]
    vz_peer = [at(((zl + k) % 4) * 4 + x, c) for k in (2, 1, 3)]
    vo_peer = [at(zl * 4 + (x + k) % 4, c) for k in (2, 1, 3)]
    vx_peer = [at(zl * 4 + (x + k) % 4, c) for k in (1, 3)]
    z_col = (1 - zh) * 8 + p

    tokens = grad.shape[0]
    first = i * EX_DEV - 1

    steps = tokens // STEP
    small = [
        pltpu.make_async_copy(src, dst, local_sem.at[n])
        for n, (src, dst) in enumerate(
            ((down_h, down), (rank_h, rank), (seg_h, seg), (sketch_h, sketch))
        )
    ]

    def block(n):
        return pl.ds(pl.multiple_of(n * STEP, STEP), STEP)

    def lat_copy(n):
        return pltpu.make_async_copy(lat_h.at[block(n), :], lat.at[block(n), :], lat_sem.at[n])

    def grad_copy(n):
        return pltpu.make_async_copy(grad_h.at[block(n), :], grad.at[block(n), :], grad_sem.at[n])

    for cp in small[:3]:
        cp.start()
    lat_copy(0).start()
    small[3].start()
    grad_copy(0).start()
    lat_copy(1).start()
    grad_copy(1).start()
    vown = pltpu.make_async_copy(val_h, vg.at[0, x], vown_sem)
    vown.start()
    barrier = pltpu.get_barrier_semaphore()
    near = p_peer + vz_peer + vo_peer + [at(above, c)]
    far = [z_peer, at(above, z_col)]
    for peer in near:
        pl.semaphore_signal(barrier, inc=1, device_id=peer, device_id_type=MESH)

    @pl.when(zh == 0)
    def _():
        for peer in far + [at(below, z_col)]:
            pl.semaphore_signal(barrier, inc=1, device_id=peer, device_id_type=MESH)

    def remote(src, dst, send, recv, peer):
        return pltpu.make_async_remote_copy(
            src_ref=src, dst_ref=dst, send_sem=send, recv_sem=recv,
            device_id=peer, device_id_type=MESH,
        )

    def drain(ref, sem):
        pltpu.make_async_copy(ref, ref, sem).wait()

    def v_begin():
        for k, peer in zip((2, 1, 3), vz_peer):
            remote(val_h, vg.at[4 - k, x], vz_send, vz_recv, peer).start()
        for peer in vo_peer:
            remote(val_h, vg.at[0, x], vo_send, vo_recv, peer).start()

    def v_turn():
        drain(vg.at[0, 0:3], vz_recv)
        for peer in vx_peer:
            remote(vg.at[1:4, x], vg.at[1:4, x], vx_send, vx_recv, peer).start()

    def v_last():
        drain(vg.at[1:4, 0:2], vx_recv)
        left, right = (x + 3) % 4, (x + 1) % 4
        for peer, source, half in ((vx_peer[0], left, pl.ds(0, 8)), (vx_peer[1], right, pl.ds(8, 8))):
            part = vg.at[1:4, source, half]
            remote(part, part, vf_send, vf_recv, peer).start()

    gp[...] = jnp.zeros_like(gp)
    side[steps - 1] = jnp.zeros((STEP, PA), BF)
    masked[steps - 1] = jnp.zeros((OWN + PB, STEP), BF)
    for cp in small:
        cp.wait()

    def project(n):
        part = jnp.dot(masked[n], side[n], preferred_element_type=F32)
        gp[0:OWN, :] += part[0:OWN]
        gp[OWN + PB : ROWS, :] += part[OWN:]

    def local_step(n, carry):
        lat_copy(n).wait()
        grad_copy(n).wait()

        @pl.when(n < steps - 2)
        def _():
            lat_copy(n + 2).start()
            grad_copy(n + 2).start()

        hidden = nt(lat[block(n), :], down[...]).astype(BF)
        out_side = jnp.dot(grad[block(n), :], sketch[...], preferred_element_type=F32)
        rank_side = lax.dot_general(
            rank[...], hidden, (((0,), (1,)), ((), ())), preferred_element_type=F32
        ).astype(BF).astype(F32)
        project(lax.rem(n + steps - 1, steps))
        ids = seg[n] - first
        for e in range(1, EX_DEV + 1):
            masked[n, (e - 1) * PB : e * PB, :] = jnp.where(ids == e, rank_side, 0.0).astype(BF)
        masked[n, OWN : OWN + PB, :] = jnp.where(ids == 0, rank_side, 0.0).astype(BF)
        side[n] = out_side.astype(BF)

        @pl.when((zh == 1) & (n == 0))
        def _():
            pl.semaphore_wait(barrier, len(near) + len(far) + 1)
            v_begin()
            for peer in far:
                pl.semaphore_signal(ready, inc=1, device_id=peer, device_id_type=MESH)

        return carry

    lax.fori_loop(0, steps, local_step, 0)
    project(steps - 1)

    for t in range(ROWS // 128):
        piece = gp[t * 128 : (t + 1) * 128, :].T
        gt[:, :, :, :, t * 128 : (t + 1) * 128] = piece.reshape(2, 4, 2, 8, 128)

    @pl.when(zh == 0)
    def _():
        pl.semaphore_wait(barrier, len(near))

    c0 = remote(gt.at[:, :, 1 - core], r0, s0_send, s0_recv, core_peer)
    c0.start()

    @pl.when(zh == 0)
    def _():
        v_begin()

    @pl.when(zh == 1)
    def _():
        v_turn()


    c0.wait_recv()
    a0[...] = gt[:, :, core] + r0[...]
    c1 = [
        remote(a0.at[:, (y + k) % 4], r1.at[k - 1], s1_send, s1_recv, peer)
        for k, peer in zip((2, 1, 3), y_peer)
    ]
    for cp in c1:
        cp.start()

    @pl.when(zh == 0)
    def _():
        v_turn()

    @pl.when(zh == 1)
    def _():
        v_last()

    drain(r1, s1_recv)
    a1[...] = (a0[:, y] + r1[0]) + (r1[1] + r1[2])
    c3 = [
        remote(a1.at[1 - zh, :, OWN:ROWS], r3.at[1], s3_send, s3_recv, at(below, z_col)),
        remote(a1.at[zh, :, OWN:ROWS], r3.at[0], s3_send, s3_recv, at(below, c)),
    ]
    c2 = remote(a1.at[1 - zh, :, 0:OWN], r2, s2_send, s2_recv, z_peer)
    @pl.when(zh == 0)
    def _():
        pl.semaphore_wait(ready, len(far))

    c3[0].start()
    c2.start()
    c3[1].start()

    @pl.when(zh == 0)
    def _():
        v_last()

    vown.wait()
    drain(vg.at[0, 0:3], vo_recv)
    drain(vg.at[1:4, 0], vf_recv)
    val = jnp.concatenate([vg[(z - zl + 4) % 4].reshape(64, 512) for z in range(4)], axis=0)
    val_hi = val.astype(BF)
    ones = jnp.ones((16, 512), BF)
    vsum = nt(ones, (val * val).astype(BF))

    c2.wait_recv()
    drain(r3, s3_recv)
    own = a1[zh, :, 0:OWN] + r2[...]
    spill = r3[0] + r3[1]
    own = jnp.concatenate([own[:, : OWN - 128], own[:, OWN - 128 :] + spill], axis=1)

    stack = jnp.concatenate([own[:, e * PB : (e + 1) * PB] for e in range(EX_DEV)], axis=0)
    wide = jnp.concatenate([stack, stack], axis=1)
    wide = jnp.concatenate([wide, wide, wide, wide], axis=1)
    row_a = lax.broadcasted_iota(jnp.int32, (EX_DEV * 8, 512), 0) % 8
    lane_a = lax.broadcasted_iota(jnp.int32, (EX_DEV * 8, 512), 1) // PB
    wide = jnp.where(row_a == lane_a, wide, 0.0)
    hi = wide.astype(BF)
    lo = (wide - hi.astype(F32)).astype(BF)
    dots = nt(jnp.concatenate([hi, lo], axis=0), val_hi)
    dots = dots[0 : EX_DEV * 8] + dots[EX_DEV * 8 :]
    dots = jnp.sum(dots.reshape(EX_DEV, 8, 256), axis=1)
    fin[:, 0:256] = dots
    fin[:, 256:384] = jnp.zeros((8, 128), F32)
    fin[0:1, 256:384] = vsum[0:1, 0:128]
    fin[1:2, 256:384] = vsum[0:1, 128:256]
    fin[2:3, 256 : 256 + EX_DEV * 8] = nt(ones, (wide * wide).astype(BF))[0:1]

    cz = remote(fin, rz, fz_send, fz_recv, z_peer)
    cz.start()
    for ref, sem in (
        (r0, s0_send), (r1, s1_send), (r2, s2_send), (r3, s3_send),
        (vg.at[0, 0:3], vz_send), (vg.at[0, 0:3], vo_send),
        (vg.at[1:4, 0:2], vx_send), (vg.at[1:4, 0], vf_send),
    ):
        drain(ref, sem)
    cz.wait_recv()
    fb[p] = fin[...] + rz[...]
    cb = [
        remote(fb.at[p], fb.at[p], fb_send, fb_recv, p_peer[k]) for k in range(7)
    ]
    for cp in cb:
        cp.start()
    drain(fb.at[0:7], fb_recv)
    total = ((fb[0] + fb[1]) + (fb[2] + fb[3])) + ((fb[4] + fb[5]) + (fb[6] + fb[7]))
    tail = total[:, 256:384]
    lanes = lax.broadcasted_iota(jnp.int32, (EX_DEV, 128), 1) // 8
    slots = lax.broadcasted_iota(jnp.int32, (EX_DEV, 128), 0)
    own_sq = jnp.sum(jnp.where(lanes == slots, tail[2:3], 0.0), axis=1, keepdims=True)
    own_scale = math.sqrt(PA * PB) * lax.rsqrt(own_sq + epsilon)
    val_scale = lax.rsqrt(tail[0:2] + epsilon)
    out_ref[:, 0:128] = total[:, 0:128] * own_scale * val_scale[0:1]
    out_ref[:, 128:256] = total[:, 128:256] * own_scale * val_scale[1:2]
    drain(rz, fz_send)
    drain(fb.at[0:7], fb_send)


def on_device(
    latent,
    adapter_down_matrix,
    output_gradient_rows,
    output_sketch_factor,
    rank_sketch_factor,
    token_example_index,
    validation_sketches,
):
    tokens, columns = output_gradient_rows.shape
    width = latent.shape[1]
    steps = tokens // STEP
    dma = pltpu.SemaphoreType.DMA
    vm = pltpu.VMEM
    return pl.pallas_call(
        kernel,
        out_shape=vm((EX_DEV, 256), F32),
        in_specs=[pl.BlockSpec(memory_space=pl.ANY)] * 7,
        out_specs=pl.BlockSpec(memory_space=pltpu.VMEM),
        scratch_shapes=[
            vm((tokens, width), BF),
            vm((PB, width), BF),
            vm((tokens, columns), BF),
            vm((columns, PA), BF),
            vm((PB, PB), BF),
            vm((steps, 1, STEP), jnp.int32),
            vm((steps, OWN + PB, STEP), BF),
            vm((steps, STEP, PA), BF),
            vm((ROWS, PA), F32),
            vm((2, 4, 2, 8, ROWS), F32),
            vm((2, 4, 8, ROWS), F32),
            vm((2, 4, 8, ROWS), F32),
            vm((3, 2, 8, ROWS), F32),
            vm((2, 8, ROWS), F32),
            vm((8, OWN), F32),
            vm((2, 8, 128), F32),
            vm((4, 4, 16, 512), F32),
            vm((8, 384), F32),
            vm((8, 384), F32),
            vm((8, 8, 384), F32),
            dma((4,)), dma((steps,)), dma((steps,)), dma,
        ] + [dma] * 8 + [pltpu.SemaphoreType.REGULAR] + [dma] * 12,
        compiler_params=pltpu.CompilerParams(
            collective_id=0, has_side_effects=True, vmem_limit_bytes=60 * 1024 * 1024
        ),
    )(
        latent,
        adapter_down_matrix,
        output_gradient_rows,
        output_sketch_factor,
        rank_sketch_factor,
        token_example_index.reshape(steps, 1, STEP),
        validation_sketches,
    )


def solution(mesh):
    in_specs = (P("dp", None), P(), P("dp", "col"), P("col", None), P(), P("dp"), P("dp", "col"))
    out_specs = P("dp", None)
    return jax.shard_map(
        on_device, mesh=mesh, in_specs=in_specs, out_specs=out_specs, check_vma=False
    )
```

profile of v0, /device:TPU:1, one launch (start us, length us, event | category | flops | bytes accessed | tf_op | source)
XLA Modules:
  0.0 32.5 jit_solution(8424016159205070768)
XLA Ops:
  0.0 31.9 %shard_map.73 = f32[8,256]{1,0:T(8,128)S(1)} custom-call(bf16[2048,512]{1,0:T(8,128)(2,1)} %lat_h.1, bf16[64,512]{1,0:T(8,128)(2,1)} %down_h.1, bf16[2048,2048]{1,0:T(8,128)(2,1)} %grad_h.1, bf16[2048,128]{1,0:T(8,128)(2,1)} %sketch_h.1, bf16[64,64]{1,0:T(8,128)(2,1)} %rank_h.1, s32[4,1,512]{2,1,0:T(1,128)} %bitcast.1, f32[16,512]{1,0:T(8,128)} %val_h.1), custom_call_target="tpu_custom_call" | custom-call | tf_op jit(solution)/shard_map/pallas_call | solution.py:299
  31.9 0.6 %copy.9 = f32[8,256]{1,0:T(8,128)} copy(f32[8,256]{1,0:T(8,128)S(1)} %shard_map.73) | data formatting | bytes 16384
where the time goes:
time: 32.6 us; the launch traced here: 32.5 us
  Pallas kernels  31.9 us (98%)
  local copies, waits for them, and re-layouts  0.6 us (2%)
    pallas_call x1, Pallas kernels, on_device(): pl.pallas_call(kernel, out_shape=vm((EX_DEV, 256), F32), in_specs=[pl.Blo...  31.9 us

commit v1 on v0

--- a/solution.py
+++ b/solution.py
@@ -32,8 +32,8 @@
 def kernel(
     lat_h, down_h, grad_h, sketch_h, rank_h, seg_h, val_h, out_ref,
     lat, down, grad, sketch, rank, seg, masked, side, gp, gt,
-    r0, a0, r1, a1, r2, r3, vg, fin, rz, fb, local_sem, lat_sem, grad_sem, vown_sem,
-    s0_send, s0_recv, s1_send, s1_recv, s2_send, s2_recv, s3_send, s3_recv,
+    r0, a0, r1, a1, r2, r3, vg, vb, fin, rz, fb, local_sem, lat_sem, grad_sem, vown_sem,
+    s0_send, s0_far, s0_near, s1_send, s1_far, s1_near, s2_send, s2_recv, s3_send, s3_recv,
     ready, vz_send, vz_recv, vo_send, vo_recv, vx_send, vx_recv, vf_send, vf_recv, fz_send, fz_recv, fb_send, fb_recv,
 ):
     i = lax.axis_index("dp")
@@ -115,12 +115,22 @@
         for peer in vx_peer:
             remote(vg.at[1:4, x], vg.at[1:4, x], vx_send, vx_recv, peer).start()
 
+    left, right, opposite = (x + 3) % 4, (x + 1) % 4, (x + 2) % 4
+
+    def v_cast(source):
+        for z in range(4):
+            vb[z, source] = vg[(z - zl + 4) % 4, source].astype(BF)
+
     def v_last():
         drain(vg.at[1:4, 0:2], vx_recv)
-        left, right = (x + 3) % 4, (x + 1) % 4
         for peer, source, half in ((vx_peer[0], left, pl.ds(0, 8)), (vx_peer[1], right, pl.ds(8, 8))):
             part = vg.at[1:4, source, half]
             remote(part, part, vf_send, vf_recv, peer).start()
+        vown.wait()
+        drain(vg.at[0, 0:3], vo_recv)
+        v_cast(x)
+        v_cast(left)
+        v_cast(right)
 
     gp[...] = jnp.zeros_like(gp)
     side[steps - 1] = jnp.zeros((STEP, PA), BF)
@@ -174,8 +184,12 @@
     def _():
         pl.semaphore_wait(barrier, len(near))
 
-    c0 = remote(gt.at[:, :, 1 - core], r0, s0_send, s0_recv, core_peer)
-    c0.start()
+    c0 = [
+        remote(gt.at[z, :, 1 - core], r0.at[z], s0_send, sem, core_peer)
+        for z, sem in ((1 - zh, s0_far), (zh, s0_near))
+    ]
+    for cp in c0:
+        cp.start()
 
     @pl.when(zh == 0)
     def _():
@@ -185,54 +199,42 @@
     def _():
         v_turn()
 
-
-    c0.wait_recv()
-    a0[...] = gt[:, :, core] + r0[...]
-    c1 = [
-        remote(a0.at[:, (y + k) % 4], r1.at[k - 1], s1_send, s1_recv, peer)
-        for k, peer in zip((2, 1, 3), y_peer)
-    ]
-    for cp in c1:
-        cp.start()
+    for n, (z, sem) in enumerate(((1 - zh, s1_far), (zh, s1_near))):
+        c0[n].wait_recv()
+        a0[z] = gt[z, :, core] + r0[z]
+        for k, peer in zip((2, 1, 3), y_peer):
+            remote(a0.at[z, (y + k) % 4], r1.at[n, k - 1], s1_send, sem, peer).start()
+
+    drain(r1.at[0], s1_far)
+    a1[0] = (a0[1 - zh, y] + r1[0, 0]) + (r1[0, 1] + r1[0, 2])
+
+    @pl.when(zh == 0)
+    def _():
+        pl.semaphore_wait(ready, len(far))
+
+    remote(a1.at[0, :, OWN:ROWS], r3.at[1], s3_send, s3_recv, at(below, z_col)).start()
+    c2 = remote(a1.at[0, :, 0:OWN], r2, s2_send, s2_recv, z_peer)
+    c2.start()
+    drain(r1.at[1], s1_near)
+    a1[1] = (a0[zh, y] + r1[1, 0]) + (r1[1, 1] + r1[1, 2])
+    remote(a1.at[1, :, OWN:ROWS], r3.at[0], s3_send, s3_recv, at(below, c)).start()
 
     @pl.when(zh == 0)
     def _():
         v_turn()
 
-    @pl.when(zh == 1)
-    def _():
-        v_last()
-
-    drain(r1, s1_recv)
-    a1[...] = (a0[:, y] + r1[0]) + (r1[1] + r1[2])
-    c3 = [
-        remote(a1.at[1 - zh, :, OWN:ROWS], r3.at[1], s3_send, s3_recv, at(below, z_col)),
-        remote(a1.at[zh, :, OWN:ROWS], r3.at[0], s3_send, s3_recv, at(below, c)),
-    ]
-    c2 = remote(a1.at[1 - zh, :, 0:OWN], r2, s2_send, s2_recv, z_peer)
-    @pl.when(zh == 0)
-    def _():
-        pl.semaphore_wait(ready, len(far))
-
-    c3[0].start()
-    c2.start()
-    c3[1].start()
-
-    @pl.when(zh == 0)
-    def _():
-        v_last()
-
-    vown.wait()
-    drain(vg.at[0, 0:3], vo_recv)
+    v_last()
+
     drain(vg.at[1:4, 0], vf_recv)
-    val = jnp.concatenate([vg[(z - zl + 4) % 4].reshape(64, 512) for z in range(4)], axis=0)
-    val_hi = val.astype(BF)
+    v_cast(opposite)
+    val_hi = vb[...].reshape(256, 512)
+    val = val_hi.astype(F32)
     ones = jnp.ones((16, 512), BF)
     vsum = nt(ones, (val * val).astype(BF))
 
     c2.wait_recv()
     drain(r3, s3_recv)
-    own = a1[zh, :, 0:OWN] + r2[...]
+    own = a1[1, :, 0:OWN] + r2[...]
     spill = r3[0] + r3[1]
     own = jnp.concatenate([own[:, : OWN - 128], own[:, OWN - 128 :] + spill], axis=1)
 
@@ -314,16 +316,17 @@
             vm((2, 4, 2, 8, ROWS), F32),
             vm((2, 4, 8, ROWS), F32),
             vm((2, 4, 8, ROWS), F32),
-            vm((3, 2, 8, ROWS), F32),
+            vm((2, 3, 8, ROWS), F32),
             vm((2, 8, ROWS), F32),
             vm((8, OWN), F32),
             vm((2, 8, 128), F32),
             vm((4, 4, 16, 512), F32),
+            vm((4, 4, 16, 512), BF),
             vm((8, 384), F32),
             vm((8, 384), F32),
             vm((8, 8, 384), F32),
             dma((4,)), dma((steps,)), dma((steps,)), dma,
-        ] + [dma] * 8 + [pltpu.SemaphoreType.REGULAR] + [dma] * 12,
+        ] + [dma] * 10 + [pltpu.SemaphoreType.REGULAR] + [dma] * 12,
         compiler_params=pltpu.CompilerParams(
             collective_id=0, has_side_effects=True, vmem_limit_bytes=60 * 1024 * 1024
         ),

time: 32.6 us -> 33.2 us (1.018)
  Pallas kernels: 31.9 us -> 32.5 us
    pallas_call x1, Pallas kernels: 31.9 us -> 32.5 us  [on_device(): pl.pallas_call(kernel, out_shape=vm((EX_DEV, 256), F32), in_specs=[pl.Blo...]
where the time goes in v1:
time: 33.2 us; the launch traced here: 33.1 us
  Pallas kernels  32.5 us (98%)
  local copies, waits for them, and re-layouts  0.6 us (2%)
    pallas_call x1, Pallas kernels, on_device(): pl.pallas_call(kernel, out_shape=vm((EX_DEV, 256), F32), in_specs=[pl.Blo...  32.5 us

profile of v1, /device:TPU:1, one launch (start us, length us, event | category | flops | bytes accessed | tf_op | source)
XLA Modules:
  0.0 33.1 jit_solution(9565065964832518766)
XLA Ops:
  0.0 32.5 %shard_map.73 = f32[8,256]{1,0:T(8,128)S(1)} custom-call(bf16[2048,512]{1,0:T(8,128)(2,1)} %lat_h.1, bf16[64,512]{1,0:T(8,128)(2,1)} %down_h.1, bf16[2048,2048]{1,0:T(8,128)(2,1)} %grad_h.1, bf16[2048,128]{1,0:T(8,128)(2,1)} %sketch_h.1, bf16[64,64]{1,0:T(8,128)(2,1)} %rank_h.1, s32[4,1,512]{2,1,0:T(1,128)} %bitcast.1, f32[16,512]{1,0:T(8,128)} %val_h.1), custom_call_target="tpu_custom_call" | custom-call | tf_op jit(solution)/shard_map/pallas_call | solution.py:301
  32.5 0.6 %copy.9 = f32[8,256]{1,0:T(8,128)} copy(f32[8,256]{1,0:T(8,128)S(1)} %shard_map.73) | data formatting | bytes 16384

commit v2 on v0

--- a/solution.py
+++ b/solution.py
@@ -34,7 +34,7 @@
     lat, down, grad, sketch, rank, seg, masked, side, gp, gt,
     r0, a0, r1, a1, r2, r3, vg, fin, rz, fb, local_sem, lat_sem, grad_sem, vown_sem,
     s0_send, s0_recv, s1_send, s1_recv, s2_send, s2_recv, s3_send, s3_recv,
-    ready, vz_send, vz_recv, vo_send, vo_recv, vx_send, vx_recv, vf_send, vf_recv, fz_send, fz_recv, fb_send, fb_recv,
+    ready, vz_send, vz_recv, vo_send, vo_recv, vx_send, vx_recv, vd_send, vd_recv, fz_send, fz_recv, fb_send, fb_recv,
 ):
     i = lax.axis_index("dp")
     c = lax.axis_index("col")
@@ -51,6 +51,7 @@
     z_peer = at(i, (1 - zh) * 8 + p)
     p_peer = [at(i, zh * 8 + (p // 2 * 2 + k) % 8 + (core + j) % 2) for k, j in FAR_FIRST]
     vz_peer = [at(((zl + k) % 4) * 4 + x, c) for k in (2, 1, 3)]
+    vd_peer = [at(((zl + k) % 4) * 4 + (x + 2) % 4, c) for k in (2, 1, 3)]
     vo_peer = [at(zl * 4 + (x + k) % 4, c) for k in (2, 1, 3)]
     vx_peer = [at(zl * 4 + (x + k) % 4, c) for k in (1, 3)]
     z_col = (1 - zh) * 8 + p
@@ -85,7 +86,7 @@
     vown = pltpu.make_async_copy(val_h, vg.at[0, x], vown_sem)
     vown.start()
     barrier = pltpu.get_barrier_semaphore()
-    near = p_peer + vz_peer + vo_peer + [at(above, c)]
+    near = p_peer + vz_peer + vo_peer + vd_peer + [at(above, c)]
     far = [z_peer, at(above, z_col)]
     for peer in near:
         pl.semaphore_signal(barrier, inc=1, device_id=peer, device_id_type=MESH)
@@ -109,18 +110,13 @@
             remote(val_h, vg.at[4 - k, x], vz_send, vz_recv, peer).start()
         for peer in vo_peer:
             remote(val_h, vg.at[0, x], vo_send, vo_recv, peer).start()
+        for k, peer in zip((2, 1, 3), vd_peer):
+            remote(val_h, vg.at[4 - k, x], vd_send, vd_recv, peer).start()
 
     def v_turn():
         drain(vg.at[0, 0:3], vz_recv)
         for peer in vx_peer:
             remote(vg.at[1:4, x], vg.at[1:4, x], vx_send, vx_recv, peer).start()
-
-    def v_last():
-        drain(vg.at[1:4, 0:2], vx_recv)
-        left, right = (x + 3) % 4, (x + 1) % 4
-        for peer, source, half in ((vx_peer[0], left, pl.ds(0, 8)), (vx_peer[1], right, pl.ds(8, 8))):
-            part = vg.at[1:4, source, half]
-            remote(part, part, vf_send, vf_recv, peer).start()
 
     gp[...] = jnp.zeros_like(gp)
     side[steps - 1] = jnp.zeros((STEP, PA), BF)
@@ -199,10 +195,6 @@
     def _():
         v_turn()
 
-    @pl.when(zh == 1)
-    def _():
-        v_last()
-
     drain(r1, s1_recv)
     a1[...] = (a0[:, y] + r1[0]) + (r1[1] + r1[2])
     c3 = [
@@ -218,13 +210,10 @@
     c2.start()
     c3[1].start()
 
-    @pl.when(zh == 0)
-    def _():
-        v_last()
-
     vown.wait()
     drain(vg.at[0, 0:3], vo_recv)
-    drain(vg.at[1:4, 0], vf_recv)
+    drain(vg.at[1:4, 0], vd_recv)
+    drain(vg.at[1:4, 0:2], vx_recv)
     val = jnp.concatenate([vg[(z - zl + 4) % 4].reshape(64, 512) for z in range(4)], axis=0)
     val_hi = val.astype(BF)
     ones = jnp.ones((16, 512), BF)
@@ -258,7 +247,7 @@
     for ref, sem in (
         (r0, s0_send), (r1, s1_send), (r2, s2_send), (r3, s3_send),
         (vg.at[0, 0:3], vz_send), (vg.at[0, 0:3], vo_send),
-        (vg.at[1:4, 0:2], vx_send), (vg.at[1:4, 0], vf_send),
+        (vg.at[1:4, 0:2], vx_send), (vg.at[1:4, 0], vd_send),
     ):
         drain(ref, sem)
     cz.wait_recv()

time: 32.6 us -> 32.5 us (level)
  Pallas kernels: 31.9 us -> 31.5 us
    pallas_call x1, Pallas kernels: 31.9 us -> 31.5 us  [on_device(): pl.pallas_call(kernel, out_shape=vm((EX_DEV, 256), F32), in_specs=[pl.Blo...]
where the time goes in v2:
time: 32.5 us; the launch traced here: 32.1 us
  Pallas kernels  31.5 us (97%)
  local copies, waits for them, and re-layouts  0.6 us (2%)
    pallas_call x1, Pallas kernels, on_device(): pl.pallas_call(kernel, out_shape=vm((EX_DEV, 256), F32), in_specs=[pl.Blo...  31.5 us

profile of v2, /device:TPU:1, one launch (start us, length us, event | category | flops | bytes accessed | tf_op | source)
XLA Modules:
  0.0 32.1 jit_solution(12523534090548279970)
XLA Ops:
  0.0 31.5 %shard_map.73 = f32[8,256]{1,0:T(8,128)S(1)} custom-call(bf16[2048,512]{1,0:T(8,128)(2,1)} %lat_h.1, bf16[64,512]{1,0:T(8,128)(2,1)} %down_h.1, bf16[2048,2048]{1,0:T(8,128)(2,1)} %grad_h.1, bf16[2048,128]{1,0:T(8,128)(2,1)} %sketch_h.1, bf16[64,64]{1,0:T(8,128)(2,1)} %rank_h.1, s32[4,1,512]{2,1,0:T(1,128)} %bitcast.1, f32[16,512]{1,0:T(8,128)} %val_h.1), custom_call_target="tpu_custom_call" | custom-call | tf_op jit(solution)/shard_map/pallas_call | solution.py:288
  31.5 0.6 %copy.9 = f32[8,256]{1,0:T(8,128)} copy(f32[8,256]{1,0:T(8,128)S(1)} %shard_map.73) | data formatting | bytes 16384

commit v3 on v1

--- a/solution.py
+++ b/solution.py
@@ -32,9 +32,9 @@
 def kernel(
     lat_h, down_h, grad_h, sketch_h, rank_h, seg_h, val_h, out_ref,
     lat, down, grad, sketch, rank, seg, masked, side, gp, gt,
-    r0, a0, r1, a1, r2, r3, vg, vb, fin, rz, fb, local_sem, lat_sem, grad_sem, vown_sem,
+    r0, a0, r1, a1, r2, r3, vg, fin, rz, fb, local_sem, lat_sem, grad_sem, vown_sem,
     s0_send, s0_far, s0_near, s1_send, s1_far, s1_near, s2_send, s2_recv, s3_send, s3_recv,
-    ready, vz_send, vz_recv, vo_send, vo_recv, vx_send, vx_recv, vf_send, vf_recv, fz_send, fz_recv, fb_send, fb_recv,
+    ready, vz_send, vz_recv, vo_send, vo_recv, vx_send, vx_recv, vd_send, vd_recv, fz_send, fz_recv, fb_send, fb_recv,
 ):
     i = lax.axis_index("dp")
     c = lax.axis_index("col")
@@ -51,6 +51,7 @@
     z_peer = at(i, (1 - zh) * 8 + p)
     p_peer = [at(i, zh * 8 + (p // 2 * 2 + k) % 8 + (core + j) % 2) for k, j in FAR_FIRST]
     vz_peer = [at(((zl + k) % 4) * 4 + x, c) for k in (2, 1, 3)]
+    vd_peer = [at(((zl + k) % 4) * 4 + (x + 2) % 4, c) for k in (2, 1, 3)]
     vo_peer = [at(zl * 4 + (x + k) % 4, c) for k in (2, 1, 3)]
     vx_peer = [at(zl * 4 + (x + k) % 4, c) for k in (1, 3)]
     z_col = (1 - zh) * 8 + p
@@ -85,7 +86,7 @@
     vown = pltpu.make_async_copy(val_h, vg.at[0, x], vown_sem)
     vown.start()
     barrier = pltpu.get_barrier_semaphore()
-    near = p_peer + vz_peer + vo_peer + [at(above, c)]
+    near = p_peer + vz_peer + vo_peer + vd_peer + [at(above, c)]
     far = [z_peer, at(above, z_col)]
     for peer in near:
         pl.semaphore_signal(barrier, inc=1, device_id=peer, device_id_type=MESH)
@@ -109,28 +110,13 @@
             remote(val_h, vg.at[4 - k, x], vz_send, vz_recv, peer).start()
         for peer in vo_peer:
             remote(val_h, vg.at[0, x], vo_send, vo_recv, peer).start()
+        for k, peer in zip((2, 1, 3), vd_peer):
+            remote(val_h, vg.at[4 - k, x], vd_send, vd_recv, peer).start()
 
     def v_turn():
         drain(vg.at[0, 0:3], vz_recv)
         for peer in vx_peer:
             remote(vg.at[1:4, x], vg.at[1:4, x], vx_send, vx_recv, peer).start()
-
-    left, right, opposite = (x + 3) % 4, (x + 1) % 4, (x + 2) % 4
-
-    def v_cast(source):
-        for z in range(4):
-            vb[z, source] = vg[(z - zl + 4) % 4, source].astype(BF)
-
-    def v_last():
-        drain(vg.at[1:4, 0:2], vx_recv)
-        for peer, source, half in ((vx_peer[0], left, pl.ds(0, 8)), (vx_peer[1], right, pl.ds(8, 8))):
-            part = vg.at[1:4, source, half]
-            remote(part, part, vf_send, vf_recv, peer).start()
-        vown.wait()
-        drain(vg.at[0, 0:3], vo_recv)
-        v_cast(x)
-        v_cast(left)
-        v_cast(right)
 
     gp[...] = jnp.zeros_like(gp)
     side[steps - 1] = jnp.zeros((STEP, PA), BF)
@@ -195,15 +181,15 @@
     def _():
         v_begin()
 
-    @pl.when(zh == 1)
-    def _():
-        v_turn()
-
     for n, (z, sem) in enumerate(((1 - zh, s1_far), (zh, s1_near))):
         c0[n].wait_recv()
         a0[z] = gt[z, :, core] + r0[z]
         for k, peer in zip((2, 1, 3), y_peer):
             remote(a0.at[z, (y + k) % 4], r1.at[n, k - 1], s1_send, sem, peer).start()
+
+    @pl.when(zh == 1)
+    def _():
+        v_turn()
 
     drain(r1.at[0], s1_far)
     a1[0] = (a0[1 - zh, y] + r1[0, 0]) + (r1[0, 1] + r1[0, 2])
@@ -223,12 +209,12 @@
     def _():
         v_turn()
 
-    v_last()
-
-    drain(vg.at[1:4, 0], vf_recv)
-    v_cast(opposite)
-    val_hi = vb[...].reshape(256, 512)
-    val = val_hi.astype(F32)
+    vown.wait()
+    drain(vg.at[0, 0:3], vo_recv)
+    drain(vg.at[1:4, 0], vd_recv)
+    drain(vg.at[1:4, 0:2], vx_recv)
+    val = jnp.concatenate([vg[(z - zl + 4) % 4].reshape(64, 512) for z in range(4)], axis=0)
+    val_hi = val.astype(BF)
     ones = jnp.ones((16, 512), BF)
     vsum = nt(ones, (val * val).astype(BF))
 
@@ -260,7 +246,7 @@
     for ref, sem in (
         (r0, s0_send), (r1, s1_send), (r2, s2_send), (r3, s3_send),
         (vg.at[0, 0:3], vz_send), (vg.at[0, 0:3], vo_send),
-        (vg.at[1:4, 0:2], vx_send), (vg.at[1:4, 0], vf_send),
+        (vg.at[1:4, 0:2], vx_send), (vg.at[1:4, 0], vd_send),
     ):
         drain(ref, sem)
     cz.wait_recv()
@@ -321,7 +307,6 @@
             vm((8, OWN), F32),
             vm((2, 8, 128), F32),
             vm((4, 4, 16, 512), F32),
-            vm((4, 4, 16, 512), BF),
             vm((8, 384), F32),
             vm((8, 384), F32),
             vm((8, 8, 384), F32),

time: 33.2 us -> 31.2 us (0.940)
  Pallas kernels: 32.5 us -> 30.5 us
    pallas_call x1, Pallas kernels: 32.5 us -> 30.5 us  [on_device(): pl.pallas_call(kernel, out_shape=vm((EX_DEV, 256), F32), in_specs=[pl.Blo...]
where the time goes in v3:
time: 31.2 us; the launch traced here: 31.1 us
  Pallas kernels  30.5 us (98%)
  local copies, waits for them, and re-layouts  0.6 us (2%)
    pallas_call x1, Pallas kernels, on_device(): pl.pallas_call(kernel, out_shape=vm((EX_DEV, 256), F32), in_specs=[pl.Blo...  30.5 us

profile of v3, /device:TPU:1, one launch (start us, length us, event | category | flops | bytes accessed | tf_op | source)
XLA Modules:
  0.0 31.1 jit_solution(513661908492050318)
XLA Ops:
  0.0 30.5 %shard_map.73 = f32[8,256]{1,0:T(8,128)S(1)} custom-call(bf16[2048,512]{1,0:T(8,128)(2,1)} %lat_h.1, bf16[64,512]{1,0:T(8,128)(2,1)} %down_h.1, bf16[2048,2048]{1,0:T(8,128)(2,1)} %grad_h.1, bf16[2048,128]{1,0:T(8,128)(2,1)} %sketch_h.1, bf16[64,64]{1,0:T(8,128)(2,1)} %rank_h.1, s32[4,1,512]{2,1,0:T(1,128)} %bitcast.1, f32[16,512]{1,0:T(8,128)} %val_h.1), custom_call_target="tpu_custom_call" | custom-call | tf_op jit(solution)/shard_map/pallas_call | solution.py:287
  30.5 0.6 %copy.9 = f32[8,256]{1,0:T(8,128)} copy(f32[8,256]{1,0:T(8,128)S(1)} %shard_map.73) | data formatting | bytes 16384

commit v4 on v3

--- a/solution.py
+++ b/solution.py
@@ -32,7 +32,7 @@
 def kernel(
     lat_h, down_h, grad_h, sketch_h, rank_h, seg_h, val_h, out_ref,
     lat, down, grad, sketch, rank, seg, masked, side, gp, gt,
-    r0, a0, r1, a1, r2, r3, vg, fin, rz, fb, local_sem, lat_sem, grad_sem, vown_sem,
+    r0, a0, r1, a1, r2, r3, vg, vb, spread_ref, fin, rz, fb, local_sem, lat_sem, grad_sem, vown_sem,
     s0_send, s0_far, s0_near, s1_send, s1_far, s1_near, s2_send, s2_recv, s3_send, s3_recv,
     ready, vz_send, vz_recv, vo_send, vo_recv, vx_send, vx_recv, vd_send, vd_recv, fz_send, fz_recv, fb_send, fb_recv,
 ):
@@ -209,37 +209,49 @@
     def _():
         v_turn()
 
+    ones = jnp.ones((16, 512), BF)
+
+    def spread():
+        c2.wait_recv()
+        drain(r3, s3_recv)
+        own = a1[1, :, 0:OWN] + r2[...]
+        spill = r3[0] + r3[1]
+        own = jnp.concatenate([own[:, : OWN - 128], own[:, OWN - 128 :] + spill], axis=1)
+        stack = jnp.concatenate([own[:, e * PB : (e + 1) * PB] for e in range(EX_DEV)], axis=0)
+        wide = jnp.concatenate([stack, stack], axis=1)
+        wide = jnp.concatenate([wide, wide, wide, wide], axis=1)
+        row_a = lax.broadcasted_iota(jnp.int32, (EX_DEV * 8, 512), 0) % 8
+        lane_a = lax.broadcasted_iota(jnp.int32, (EX_DEV * 8, 512), 1) // PB
+        wide = jnp.where(row_a == lane_a, wide, 0.0)
+        hi = wide.astype(BF)
+        spread_ref[0 : EX_DEV * 8, :] = hi
+        spread_ref[EX_DEV * 8 :, :] = (wide - hi.astype(F32)).astype(BF)
+        fin[2:3, 256 : 256 + EX_DEV * 8] = nt(ones, (wide * wide).astype(BF))[0:1]
+
+    fin[:, 256:384] = jnp.zeros((8, 128), F32)
+
+    @pl.when(zh == 1)
+    def _():
+        spread()
+
     vown.wait()
     drain(vg.at[0, 0:3], vo_recv)
     drain(vg.at[1:4, 0], vd_recv)
     drain(vg.at[1:4, 0:2], vx_recv)
     val = jnp.concatenate([vg[(z - zl + 4) % 4].reshape(64, 512) for z in range(4)], axis=0)
     val_hi = val.astype(BF)
-    ones = jnp.ones((16, 512), BF)
+    vb[...] = val_hi
     vsum = nt(ones, (val * val).astype(BF))
-
-    c2.wait_recv()
-    drain(r3, s3_recv)
-    own = a1[1, :, 0:OWN] + r2[...]
-    spill = r3[0] + r3[1]
-    own = jnp.concatenate([own[:, : OWN - 128], own[:, OWN - 128 :] + spill], axis=1)
-
-    stack = jnp.concatenate([own[:, e * PB : (e + 1) * PB] for e in range(EX_DEV)], axis=0)
-    wide = jnp.concatenate([stack, stack], axis=1)
-    wide = jnp.concatenate([wide, wide, wide, wide], axis=1)
-    row_a = lax.broadcasted_iota(jnp.int32, (EX_DEV * 8, 512), 0) % 8
-    lane_a = lax.broadcasted_iota(jnp.int32, (EX_DEV * 8, 512), 1) // PB
-    wide = jnp.where(row_a == lane_a, wide, 0.0)
-    hi = wide.astype(BF)
-    lo = (wide - hi.astype(F32)).astype(BF)
-    dots = nt(jnp.concatenate([hi, lo], axis=0), val_hi)
-    dots = dots[0 : EX_DEV * 8] + dots[EX_DEV * 8 :]
-    dots = jnp.sum(dots.reshape(EX_DEV, 8, 256), axis=1)
-    fin[:, 0:256] = dots
-    fin[:, 256:384] = jnp.zeros((8, 128), F32)
     fin[0:1, 256:384] = vsum[0:1, 0:128]
     fin[1:2, 256:384] = vsum[0:1, 128:256]
-    fin[2:3, 256 : 256 + EX_DEV * 8] = nt(ones, (wide * wide).astype(BF))[0:1]
+
+    @pl.when(zh == 0)
+    def _():
+        spread()
+
+    dots = nt(spread_ref[...], vb[...])
+    dots = dots[0 : EX_DEV * 8] + dots[EX_DEV * 8 :]
+    fin[:, 0:256] = jnp.sum(dots.reshape(EX_DEV, 8, 256), axis=1)
 
     cz = remote(fin, rz, fz_send, fz_recv, z_peer)
     cz.start()
@@ -307,6 +319,8 @@
             vm((8, OWN), F32),
             vm((2, 8, 128), F32),
             vm((4, 4, 16, 512), F32),
+            vm((256, 512), BF),
+            vm((2 * EX_DEV * 8, 512), BF),
             vm((8, 384), F32),
             vm((8, 384), F32),
             vm((8, 8, 384), F32),

time: 31.2 us -> 31.5 us (level)
  Pallas kernels: 30.5 us -> 30.9 us
    pallas_call x1, Pallas kernels: 30.5 us -> 30.9 us  [on_device(): pl.pallas_call(kernel, out_shape=vm((EX_DEV, 256), F32), in_specs=[pl.Blo...]
where the time goes in v4:
time: 31.5 us
  Pallas kernels  30.9 us (98%)
  local copies, waits for them, and re-layouts  0.6 us (2%)
    pallas_call x1, Pallas kernels, on_device(): pl.pallas_call(kernel, out_shape=vm((EX_DEV, 256), F32), in_specs=[pl.Blo...  30.9 us

profile of v4, /device:TPU:1, one launch (start us, length us, event | category | flops | bytes accessed | tf_op | source)
XLA Modules:
  0.0 31.5 jit_solution(7562971284141392249)
XLA Ops:
  0.0 30.9 %shard_map.73 = f32[8,256]{1,0:T(8,128)S(1)} custom-call(bf16[2048,512]{1,0:T(8,128)(2,1)} %lat_h.1, bf16[64,512]{1,0:T(8,128)(2,1)} %down_h.1, bf16[2048,2048]{1,0:T(8,128)(2,1)} %grad_h.1, bf16[2048,128]{1,0:T(8,128)(2,1)} %sketch_h.1, bf16[64,64]{1,0:T(8,128)(2,1)} %rank_h.1, s32[4,1,512]{2,1,0:T(1,128)} %bitcast.1, f32[16,512]{1,0:T(8,128)} %val_h.1), custom_call_target="tpu_custom_call" | custom-call | tf_op jit(solution)/shard_map/pallas_call | solution.py:299
  30.9 0.6 %copy.9 = f32[8,256]{1,0:T(8,128)} copy(f32[8,256]{1,0:T(8,128)S(1)} %shard_map.73) | data formatting | bytes 16384

commit v5 on v4

--- a/solution.py
+++ b/solution.py
@@ -18,7 +18,8 @@
 BF = jnp.bfloat16
 F32 = jnp.float32
 
-STEP = 512
+STEP = 256
+AHEAD = 4
 OWN = EX_DEV * PB
 ROWS = OWN + 2 * PB
 
@@ -81,8 +82,9 @@
     lat_copy(0).start()
     small[3].start()
     grad_copy(0).start()
-    lat_copy(1).start()
-    grad_copy(1).start()
+    for n in range(1, AHEAD):
+        lat_copy(n).start()
+        grad_copy(n).start()
     vown = pltpu.make_async_copy(val_h, vg.at[0, x], vown_sem)
     vown.start()
     barrier = pltpu.get_barrier_semaphore()
@@ -133,10 +135,10 @@
         lat_copy(n).wait()
         grad_copy(n).wait()
 
-        @pl.when(n < steps - 2)
+        @pl.when(n < steps - AHEAD)
         def _():
-            lat_copy(n + 2).start()
-            grad_copy(n + 2).start()
+            lat_copy(n + AHEAD).start()
+            grad_copy(n + AHEAD).start()
 
         hidden = nt(lat[block(n), :], down[...]).astype(BF)
         out_side = jnp.dot(grad[block(n), :], sketch[...], preferred_element_type=F32)
@@ -150,7 +152,7 @@
         masked[n, OWN : OWN + PB, :] = jnp.where(ids == 0, rank_side, 0.0).astype(BF)
         side[n] = out_side.astype(BF)
 
-        @pl.when((zh == 1) & (n == 0))
+        @pl.when((zh == 1) & (n == 1))
         def _():
             pl.semaphore_wait(barrier, len(near) + len(far) + 1)
             v_begin()

time: 31.5 us -> 32.5 us (1.032)
  Pallas kernels: 30.9 us -> 31.8 us
    pallas_call x1, Pallas kernels: 30.9 us -> 31.8 us  [on_device(): pl.pallas_call(kernel, out_shape=vm((EX_DEV, 256), F32), in_specs=[pl.Blo...]
where the time goes in v5:
time: 32.5 us; the launch traced here: 32.4 us
  Pallas kernels  31.8 us (98%)
  local copies, waits for them, and re-layouts  0.6 us (2%)
    pallas_call x1, Pallas kernels, on_device(): pl.pallas_call(kernel, out_shape=vm((EX_DEV, 256), F32), in_specs=[pl.Blo...  31.8 us

profile of v5, /device:TPU:1, one launch (start us, length us, event | category | flops | bytes accessed | tf_op | source)
XLA Modules:
  0.0 32.4 jit_solution(3046114367374592353)
XLA Ops:
  0.0 31.8 %shard_map.73 = f32[8,256]{1,0:T(8,128)S(1)} custom-call(bf16[2048,512]{1,0:T(8,128)(2,1)} %lat_h.1, bf16[64,512]{1,0:T(8,128)(2,1)} %down_h.1, bf16[2048,2048]{1,0:T(8,128)(2,1)} %grad_h.1, bf16[2048,128]{1,0:T(8,128)(2,1)} %sketch_h.1, bf16[64,64]{1,0:T(8,128)(2,1)} %rank_h.1, s32[8,1,256]{2,1,0:T(1,128)} %bitcast.1, f32[16,512]{1,0:T(8,128)} %val_h.1), custom_call_target="tpu_custom_call" | custom-call | tf_op jit(solution)/shard_map/pallas_call | solution.py:301
  31.8 0.6 %copy.9 = f32[8,256]{1,0:T(8,128)} copy(f32[8,256]{1,0:T(8,128)S(1)} %shard_map.73) | data formatting | bytes 16384

commit v6 on v4

--- a/solution.py
+++ b/solution.py
@@ -129,6 +129,8 @@
         gp[0:OWN, :] += part[0:OWN]
         gp[OWN + PB : ROWS, :] += part[OWN:]
 
+    early = jnp.where(x + y < 3, 1, 0)
+
     def local_step(n, carry):
         lat_copy(n).wait()
         grad_copy(n).wait()
@@ -150,7 +152,7 @@
         masked[n, OWN : OWN + PB, :] = jnp.where(ids == 0, rank_side, 0.0).astype(BF)
         side[n] = out_side.astype(BF)
 
-        @pl.when((zh == 1) & (n == 0))
+        @pl.when((zh == 1) & (n == early))
         def _():
             pl.semaphore_wait(barrier, len(near) + len(far) + 1)
             v_begin()

time: 31.5 us -> 31.5 us (level)
  no operation moved by 1% of the time
where the time goes in v6:
time: 31.5 us
  Pallas kernels  30.9 us (98%)
  local copies, waits for them, and re-layouts  0.6 us (2%)
    pallas_call x1, Pallas kernels, on_device(): pl.pallas_call(kernel, out_shape=vm((EX_DEV, 256), F32), in_specs=[pl.Blo...  30.9 us

profile of v6, /device:TPU:1, one launch (start us, length us, event | category | flops | bytes accessed | tf_op | source)
XLA Modules:
  0.0 31.5 jit_solution(4489317910402660174)
XLA Ops:
  0.0 30.9 %shard_map.73 = f32[8,256]{1,0:T(8,128)S(1)} custom-call(bf16[2048,512]{1,0:T(8,128)(2,1)} %lat_h.1, bf16[64,512]{1,0:T(8,128)(2,1)} %down_h.1, bf16[2048,2048]{1,0:T(8,128)(2,1)} %grad_h.1, bf16[2048,128]{1,0:T(8,128)(2,1)} %sketch_h.1, bf16[64,64]{1,0:T(8,128)(2,1)} %rank_h.1, s32[4,1,512]{2,1,0:T(1,128)} %bitcast.1, f32[16,512]{1,0:T(8,128)} %val_h.1), custom_call_target="tpu_custom_call" | custom-call | tf_op jit(solution)/shard_map/pallas_call | solution.py:301
  30.9 0.6 %copy.9 = f32[8,256]{1,0:T(8,128)} copy(f32[8,256]{1,0:T(8,128)S(1)} %shard_map.73) | data formatting | bytes 16384

commit v7 on v4

--- a/solution.py
+++ b/solution.py
@@ -160,11 +160,13 @@
         return carry
 
     lax.fori_loop(0, steps, local_step, 0)
-    project(steps - 1)
-
-    for t in range(ROWS // 128):
-        piece = gp[t * 128 : (t + 1) * 128, :].T
-        gt[:, :, :, :, t * 128 : (t + 1) * 128] = piece.reshape(2, 4, 2, 8, 128)
+    part = jnp.dot(masked[steps - 1], side[steps - 1], preferred_element_type=F32)
+    for t in range(OWN // 128):
+        span = slice(t * 128, (t + 1) * 128)
+        gt[:, :, :, :, span] = (gp[span, :] + part[span]).T.reshape(2, 4, 2, 8, 128)
+    spill = gp[OWN + PB : ROWS, :] + part[OWN:]
+    spill = jnp.concatenate([jnp.zeros((PB, PA), F32), spill], axis=0)
+    gt[:, :, :, :, OWN:ROWS] = spill.T.reshape(2, 4, 2, 8, 128)
 
     @pl.when(zh == 0)
     def _():

time: 31.5 us -> 31.5 us (level)
  no operation moved by 1% of the time
where the time goes in v7:
time: 31.5 us
  Pallas kernels  30.9 us (98%)
  local copies, waits for them, and re-layouts  0.6 us (2%)
    pallas_call x1, Pallas kernels, on_device(): pl.pallas_call(kernel, out_shape=vm((EX_DEV, 256), F32), in_specs=[pl.Blo...  30.9 us

profile of v7, /device:TPU:1, one launch (start us, length us, event | category | flops | bytes accessed | tf_op | source)
XLA Modules:
  0.0 31.5 jit_solution(1860633052966535801)
XLA Ops:
  0.0 30.9 %shard_map.73 = f32[8,256]{1,0:T(8,128)S(1)} custom-call(bf16[2048,512]{1,0:T(8,128)(2,1)} %lat_h.1, bf16[64,512]{1,0:T(8,128)(2,1)} %down_h.1, bf16[2048,2048]{1,0:T(8,128)(2,1)} %grad_h.1, bf16[2048,128]{1,0:T(8,128)(2,1)} %sketch_h.1, bf16[64,64]{1,0:T(8,128)(2,1)} %rank_h.1, s32[4,1,512]{2,1,0:T(1,128)} %bitcast.1, f32[16,512]{1,0:T(8,128)} %val_h.1), custom_call_target="tpu_custom_call" | custom-call | tf_op jit(solution)/shard_map/pallas_call | solution.py:301
  30.9 0.6 %copy.9 = f32[8,256]{1,0:T(8,128)} copy(f32[8,256]{1,0:T(8,128)S(1)} %shard_map.73) | data formatting | bytes 16384
